TPU v7x, 32 devices: a whole 2x2x4 slice. The times are simulated.
32 devices in a mesh: parts: 2 (over x), tm: 8 (over z, y), panel: 2 (over core).
Axes of the slice: x: 2, y: 2, z: 4, core: 2. Of those that a mesh axis runs over, the one named last changes fastest.
Arguments:
- gain: bfloat16 [16, 1024, 1024], P(('parts', 'tm'), 'panel'), parts along dimension 0, may hold values from -0.1875 to 0.1875
- offset: bfloat16 [16, 1024], P(('parts', 'tm')), parts along dimension 0, may hold values from -3 to 3
- residual_cov: bfloat16 [16, 1024, 1024], P(('parts', 'tm'), 'panel'), parts along dimension 0, may hold values from -9 to 9, as said below
Outputs:
- smoothed_mean: bfloat16 [16, 1024], P(('parts', 'tm')), parts along dimension 0
- smoothed_cov: bfloat16 [16, 1024, 1024], P(('parts', 'tm'), 'panel'), parts along dimension 0
There are 2 independent parts, one for each index of `parts`. A program takes and returns all parts, laid end to end along the dimension named above; each array names one. Nothing has to cross between parts.
Inputs may be any that keep to these rules, and one draw needn't show every extreme that they name: Each block residual_cov[k] is a symmetric matrix.
All inputs are finite; a program needn't handle non-finite values.
Results may differ from a plain program's by a relative error of at most 0.0062.
Values may be sent and summed in bfloat16 or wider, within the bound.
A program may use at most 128 MiB of HBM per device.

v0:
```python
import jax
import jax.numpy as jnp
from jax import lax
from jax.sharding import PartitionSpec as P


def shifted(block, axis, distance):
    devices = range(lax.axis_size(axis))
    route = [(i - distance, i) for i in devices if i - distance in devices]
    return lax.ppermute(block, axis, route)


def times_transposed(left, right):
    return lax.dot_general(
        left, right, (((1,), (1,)), ((), ())), preferred_element_type=jnp.float32
    )


def body(gain, offset, residual_cov):
    is_last = lax.axis_index("tm") == lax.axis_size("tm") - 1
    own_gain = jnp.where(is_last, jnp.zeros_like(gain[0]), gain[0])
    own_cov = residual_cov[0]
    own_offset = offset[0]
    levels = (lax.axis_size("tm") - 1).bit_length()
    for level in range(levels):
        final = level == levels - 1
        far_pair, far_offset = shifted(
            (jnp.stack([own_gain, own_cov]), own_offset), "tm", -(1 << level)
        )
        needed = far_pair[1:] if final else far_pair
        whole_own, whole_far = (
            lax.all_gather(own_gain, "panel", axis=0, tiled=True),
            lax.all_gather(needed, "panel", axis=1, tiled=True),
        )
        cross = jnp.dot(own_gain, whole_far[-1], preferred_element_type=jnp.float32).astype(
            jnp.bfloat16
        )
        new_cov = (times_transposed(cross, whole_own) + own_cov.astype(jnp.float32)).astype(
            jnp.bfloat16
        )
        new_offset = (
            jnp.dot(whole_own, far_offset, preferred_element_type=jnp.float32)
            + own_offset.astype(jnp.float32)
        ).astype(jnp.bfloat16)
        if not final:
            own_gain = jnp.dot(own_gain, whole_far[0], preferred_element_type=jnp.float32).astype(
                jnp.bfloat16
            )
        own_cov = new_cov
        own_offset = new_offset
    return (own_offset[None], own_cov[None])


def solution(mesh):
    in_specs = (
        P(("parts", "tm"), "panel", None),
        P(("parts", "tm"), None),
        P(("parts", "tm"), "panel", None),
    )
    out_specs = (P(("parts", "tm"), None), P(("parts", "tm"), "panel", None))
    return jax.shard_map(body, mesh=mesh, in_specs=in_specs, out_specs=out_specs, check_vma=False)
```

profile of v0, /device:TPU:5, one launch (start us, length us, event | category | flops | bytes accessed | tf_op | source)
XLA Modules:
  0.0 310.7 jit_solution(10901256251537795429)
XLA Ops:
  9.6 1.9 collective-permute-start
  11.5 47.4 %collective-permute-done = bf16[2,512,1024]{2,1,0:T(8,128)(2,1)S(1)} collective-permute-done((bf16[2,512,1024]{2,1,0:T(8,128)(2,1)S(1)}, bf16[2,512,1024]{2,1,0:T(8,128)(2,1)S(1)}, u32[]{:S(2)}, u32[]{:S(2)}) %collective-permute-start) | collective-permute-done | bytes 2097184 | tf_op jit(solution)/shard_map/ppermute | solution.py:10
  58.9 1.4 copy-done.9
  61.1 14.8 %all-gather.8.cloned.1.call-done = bf16[2,1024,1024]{2,1,0:T(8,128)(2,1)} async-done(((bf16[2,512,1024]{2,1,0:T(8,128)(2,1)}), bf16[2,1024,1024]{2,1,0:T(8,128)(2,1)}) %all-gather.8.cloned.1.call-update) | async-done | bytes 4194320 | tf_op jit(solution)/shard_map/all_gather | solution.py:33
  75.9 2.8 fusion.14
  78.8 11.0 %all-gather.18.cloned.1.call-done = bf16[1,1024,1024]{2,1,0:T(8,128)(2,1)} async-done(((bf16[1,512,1024]{2,1,0:T(8,128)(2,1)}), bf16[1,1024,1024]{2,1,0:T(8,128)(2,1)}) %all-gather.18.cloned.1.call-update) | async-done | bytes 2097168 | tf_op jit(solution)/shard_map/all_gather | solution.py:32
  89.8 5.5 %fusion.4 = bf16[512,1024]{1,0:T(8,128)(2,1)} fusion(bf16[1,1024,1024]{2,1,0:T(8,128)(2,1)} %all-gather.18.cloned.1.call-done, bf16[1,512,1024]{2,1,0:T(8,128)(2,1)S(1)} %copy-done.12, bf16[2,1024,1024]{2,1,0:T(8,128)(2,1)} %all-gather.8.cloned.1.call-done, bf16[1,512,1024]{2,1,0:T(8,128)(2,1)S(1)} %copy-done.1), kind=kOutput, calls=%fused_computation.12 | convolution fusion | flops 2149580800 | bytes 7340032 | tf_op jit(solution)/shard_map/dot_general | solution.py:14
  95.3 1.4 pad_maximum_fusion.1
  96.8 1.4 collective-permute-start.1
  98.2 47.6 %collective-permute-done.1 = bf16[2,512,1024]{2,1,0:T(8,128)(2,1)S(1)} collective-permute-done((bf16[2,512,1024]{2,1,0:T(8,128)(2,1)S(1)}, bf16[2,512,1024]{2,1,0:T(8,128)(2,1)S(1)}, u32[]{:S(2)}, u32[]{:S(2)}) %collective-permute-start.1) | collective-permute-done | bytes 2097184 | tf_op jit(solution)/shard_map/ppermute | solution.py:10
  147.9 14.3 %all-gather.10.cloned.1.call-done = bf16[2,1024,1024]{2,1,0:T(8,128)(2,1)} async-done(((bf16[2,512,1024]{2,1,0:T(8,128)(2,1)}), bf16[2,1024,1024]{2,1,0:T(8,128)(2,1)}) %all-gather.10.cloned.1.call-update) | async-done | bytes 4194320 | tf_op jit(solution)/shard_map/all_gather | solution.py:33
  162.1 2.8 fusion.16
  165.0 10.3 %all-gather.14.cloned.1.call-done = bf16[1024,1024]{1,0:T(8,128)(2,1)} async-done(((bf16[512,1024]{1,0:T(8,128)(2,1)}), bf16[1024,1024]{1,0:T(8,128)(2,1)}) %all-gather.14.cloned.1.call-update) | async-done | bytes 2097168 | tf_op jit(solution)/shard_map/all_gather | solution.py:32
  175.3 4.8 %add_convert_fusion.1 = bf16[512,1024]{1,0:T(8,128)(2,1)S(1)} fusion(bf16[512,1024]{1,0:T(8,128)(2,1)} %fusion.4, bf16[1024,1024]{1,0:T(8,128)(2,1)} %all-gather.14.cloned.1.call-done, bf16[512,1024]{1,0:T(8,128)(2,1)S(1)} %copy-done.5, bf16[2,1024,1024]{2,1,0:T(8,128)(2,1)} %all-gather.10.cloned.1.call-done), kind=kOutput, calls=%fused_computation.20 | convolution fusion | flops 2149580800 | bytes 7340032 | tf_op jit(solution)/shard_map/dot_general | solution.py:14
  180.1 1.7 pad_maximum_fusion.2
  181.8 1.4 collective-permute-start.5
  183.3 93.7 %collective-permute-done.5 = bf16[2,512,1024]{2,1,0:T(8,128)(2,1)} collective-permute-done((bf16[2,512,1024]{2,1,0:T(8,128)(2,1)}, bf16[2,512,1024]{2,1,0:T(8,128)(2,1)}, u32[]{:S(2)}, u32[]{:S(2)}) %collective-permute-start.5) | collective-permute-done | bytes 2097184 | tf_op jit(solution)/shard_map/ppermute | solution.py:10
  277.0 2.3 slice.24
  279.4 2.1 collective-permute-start.2
  281.5 3.3 %collective-permute-done.2 = bf16[1024]{0:T(1024)(128)(2,1)S(1)} collective-permute-done((bf16[1024]{0:T(1024)(128)(2,1)S(1)}, bf16[1024]{0:T(1024)(128)(2,1)S(1)}, u32[]{:S(2)}, u32[]{:S(2)}) %collective-permute-start.2) | collective-permute-done | bytes 2080 | tf_op jit(solution)/shard_map/ppermute | solution.py:10
  286.7 3.0 collective-permute-done.3
  291.8 3.9 %collective-permute-done.4 = bf16[1024]{0:T(1024)(128)(2,1)S(1)} collective-permute-done((bf16[1024]{0:T(1024)(128)(2,1)S(1)}, bf16[1024]{0:T(1024)(128)(2,1)S(1)}, u32[]{:S(2)}, u32[]{:S(2)}) %collective-permute-start.4) | collective-permute-done | bytes 2080 | tf_op jit(solution)/shard_map/ppermute | solution.py:10
  295.7 2.4 fusion.28
  298.7 5.2 %fusion.20 = bf16[1,512,1024]{2,1,0:T(8,128)(2,1)} fusion(bf16[512,1024]{1,0:T(8,128)(2,1)} %copy-done.13, bf16[1024,1024]{1,0:T(8,128)(2,1)S(1)} %copy-done.7, bf16[512,1024]{1,0:T(8,128)(2,1)S(1)} %copy-done.3, bf16[1,1024,1024]{2,1,0:T(8,128)(2,1)} %all-gather.16.cloned.1.call-done), kind=kOutput, calls=%fused_computation.26 | convolution fusion | flops 2149580800 | bytes 7340032 | tf_op jit(solution)/shard_map/dot_general | solution.py:14
  (57 shorter events, 9.9 us)
Async XLA Ops:
  7.2 1.5 copy-start.11
  7.2 68.7 %all-gather.8.cloned.1.call-start = ((), (), s32[]{:S(2)}) async-start(), calls=%async_computation | async-start | bytes 6291456 | tf_op jit(solution)/shard_map/all_gather | solution.py:33
  9.6 49.3 %collective-permute-start = (bf16[2,512,1024]{2,1,0:T(8,128)(2,1)S(1)}, bf16[2,512,1024]{2,1,0:T(8,128)(2,1)S(1)}, u32[]{:S(2)}, u32[]{:S(2)}) collective-permute-start(bf16[2,512,1024]{2,1,0:T(8,128)(2,1)S(1)} %pad_maximum_fusion), channel_id=1, source_target_pairs={{2,0},{4,2},{6,4},{8,6},{10,8},{12,10},{14,12},{3,1},{5,3},{7,5},{... | collective-permute-start | bytes 6291464 | tf_op jit(solution)/shard_map/ppermute | solution.py:10
  11.5 64.4 %copy-start.1 = (bf16[1,512,1024]{2,1,0:T(8,128)(2,1)S(1)}, bf16[1,512,1024]{2,1,0:T(8,128)(2,1)}, u32[]{:S(2)}) copy-start(bf16[1,512,1024]{2,1,0:T(8,128)(2,1)} %copy-done) | copy-start | bytes 3145732
  60.3 29.5 %all-gather.18.cloned.1.call-start = ((), (), s32[]{:S(2)}) async-start(), calls=%async_computation.5 | async-start | bytes 3145728 | tf_op jit(solution)/shard_map/all_gather | solution.py:32
  61.0 28.8 %copy-start.12 = (bf16[1,512,1024]{2,1,0:T(8,128)(2,1)S(1)}, bf16[1,512,1024]{2,1,0:T(8,128)(2,1)}, u32[]{:S(2)}) copy-start(bf16[1,512,1024]{2,1,0:T(8,128)(2,1)} %param.5) | copy-start | bytes 3145732
  61.1 101.1 %all-gather.10.cloned.1.call-start = ((), (), s32[]{:S(2)}) async-start(), calls=%async_computation.1 | async-start | bytes 6291456 | tf_op jit(solution)/shard_map/all_gather | solution.py:33
  78.8 16.6 %copy-start.4 = (bf16[512,1024]{1,0:T(8,128)(2,1)}, bf16[512,1024]{1,0:T(8,128)(2,1)S(1)}, u32[]{:S(2)}) copy-start(bf16[512,1024]{1,0:T(8,128)(2,1)S(1)} %fusion.14) | copy-start | bytes 3145732
  96.8 65.4 %copy-start.5 = (bf16[512,1024]{1,0:T(8,128)(2,1)S(1)}, bf16[512,1024]{1,0:T(8,128)(2,1)}, u32[]{:S(2)}) copy-start(bf16[512,1024]{1,0:T(8,128)(2,1)} %copy-done.4) | copy-start | bytes 3145732
  96.8 49.0 %collective-permute-start.1 = (bf16[2,512,1024]{2,1,0:T(8,128)(2,1)S(1)}, bf16[2,512,1024]{2,1,0:T(8,128)(2,1)S(1)}, u32[]{:S(2)}, u32[]{:S(2)}) collective-permute-start(bf16[2,512,1024]{2,1,0:T(8,128)(2,1)S(1)} %pad_maximum_fusion.1), channel_id=1, source_target_pairs={{4,0},{6,2},{8,4},{10,6},{12,8},{14,10},{5,1},{7,3},{9,5},{11,7},{... | collective-permute-start | bytes 6291464 | tf_op jit(solution)/shard_map/ppermute | solution.py:10
  147.2 28.1 %all-gather.14.cloned.1.call-start = ((), (), s32[]{:S(2)}) async-start(), calls=%async_computation.3 | async-start | bytes 3145728 | tf_op jit(solution)/shard_map/all_gather | solution.py:32
  147.8 147.9 %all-gather.12.cloned.1.call-start = ((), (), s32[]{:S(2)}) async-start(), calls=%async_computation.2 | async-start | bytes 3145728 | tf_op jit(solution)/shard_map/all_gather | solution.py:32
  165.0 15.2 %copy-start.2 = (bf16[512,1024]{1,0:T(8,128)(2,1)}, bf16[512,1024]{1,0:T(8,128)(2,1)S(1)}, u32[]{:S(2)}) copy-start(bf16[512,1024]{1,0:T(8,128)(2,1)S(1)} %fusion.16) | copy-start | bytes 3145732
  180.1 110.3 %copy-start.13 = (bf16[512,1024]{1,0:T(8,128)(2,1)}, bf16[512,1024]{1,0:T(8,128)(2,1)S(1)}, u32[]{:S(2)}) copy-start(bf16[512,1024]{1,0:T(8,128)(2,1)S(1)} %add_convert_fusion.1) | copy-start | bytes 3145732
  181.8 97.5 %copy-start.14 = (bf16[1,1024]{1,0:T(2,128)(2,1)S(1)}, bf16[1,1024]{1,0:T(2,128)(2,1)}, u32[]{:S(2)}) copy-start(bf16[1,1024]{1,0:T(2,128)(2,1)} %param.4) | copy-start | bytes 6148
  181.8 102.9 %copy-start.6 = (bf16[1,1024,1024]{2,1,0:T(8,128)(2,1)S(1)}, bf16[1,1024,1024]{2,1,0:T(8,128)(2,1)}, u32[]{:S(2)}) copy-start(bf16[1,1024,1024]{2,1,0:T(8,128)(2,1)} %all-gather.18.cloned.1.call-done) | copy-start | bytes 6291460
  181.8 95.2 %collective-permute-start.5 = (bf16[2,512,1024]{2,1,0:T(8,128)(2,1)}, bf16[2,512,1024]{2,1,0:T(8,128)(2,1)}, u32[]{:S(2)}, u32[]{:S(2)}) collective-permute-start(bf16[2,512,1024]{2,1,0:T(8,128)(2,1)} %pad_maximum_fusion.2), channel_id=1, source_target_pairs={{8,0},{10,2},{12,4},{14,6},{9,1},{11,3},{13,5},{15,7},{24,16},{26,... | collective-permute-start | bytes 6291464 | tf_op jit(solution)/shard_map/ppermute | solution.py:10
  183.3 115.4 %all-gather.16.cloned.1.call-start = ((), (), s32[]{:S(2)}) async-start(), calls=%async_computation.4 | async-start | bytes 3145728 | tf_op jit(solution)/shard_map/all_gather | solution.py:33
  279.4 10.4 %copy-start.8 = (bf16[1024,1024]{1,0:T(8,128)(2,1)S(1)}, bf16[1024,1024]{1,0:T(8,128)(2,1)}, u32[]{:S(2)}) copy-start(bf16[1024,1024]{1,0:T(8,128)(2,1)} %all-gather.14.cloned.1.call-done) | copy-start | bytes 6291460
  279.4 5.4 %collective-permute-start.2 = (bf16[1024]{0:T(1024)(128)(2,1)S(1)}, bf16[1024]{0:T(1024)(128)(2,1)S(1)}, u32[]{:S(2)}, u32[]{:S(2)}) collective-permute-start(bf16[1024]{0:T(1024)(128)(2,1)S(1)} %reduce), channel_id=1, source_target_pairs={{2,0},{4,2},{6,4},{8,6},{10,8},{12,10},{14,12},{3,1},{5,3},{7,5},{... | collective-permute-start | bytes 6152 | tf_op jit(solution)/shard_map/ppermute | solution.py:10
  285.4 4.3 %collective-permute-start.3 = (bf16[1024]{0:T(1024)(128)(2,1)S(1)}, bf16[1024]{0:T(1024)(128)(2,1)S(1)}, u32[]{:S(2)}, u32[]{:S(2)}) collective-permute-start(bf16[1024]{0:T(1024)(128)(2,1)S(1)} %add_convert_fusion.4), channel_id=1, source_target_pairs={{4,0},{6,2},{8,4},{10,6},{12,8},{14,10},{5,1},{7,3},{9,5},{11,7},{... | collective-permute-start | bytes 6152 | tf_op jit(solution)/shard_map/ppermute | solution.py:10
  289.8 8.9 %copy-start.3 = (bf16[512,1024]{1,0:T(8,128)(2,1)S(1)}, bf16[512,1024]{1,0:T(8,128)(2,1)}, u32[]{:S(2)}) copy-start(bf16[512,1024]{1,0:T(8,128)(2,1)} %copy-done.2) | copy-start | bytes 3145732
  290.5 5.2 %collective-permute-start.4 = (bf16[1024]{0:T(1024)(128)(2,1)S(1)}, bf16[1024]{0:T(1024)(128)(2,1)S(1)}, u32[]{:S(2)}, u32[]{:S(2)}) collective-permute-start(bf16[1024]{0:T(1024)(128)(2,1)S(1)} %add_convert_fusion.3), channel_id=1, source_target_pairs={{8,0},{10,2},{12,4},{14,6},{9,1},{11,3},{13,5},{15,7},{24,16},{26,... | collective-permute-start | bytes 6152 | tf_op jit(solution)/shard_map/ppermute | solution.py:10
  295.7 3.0 copy-start.7
  (3 other events, 3.8 us)
Sparse Core Ops, SparseCore 0:
  60.4 15.4 all-gather.7
  78.0 11.7 all-gather.17
  147.3 14.7 all-gather.9
  163.5 11.7 all-gather.13
  183.4 14.1 all-gather.11
  279.5 9.7 all-gather.15
where the time goes:
time: 315 us; the launch traced here: 311 us
  waiting for transfers between devices  251 us (80%)
  matrix products  24.9 us (8%)
  between operations  14.3 us (5%)
  starting transfers between devices  9.62 us (3%)
  local copies, waits for them, and re-layouts  6.54 us (2%)
  other arithmetic  4.74 us (2%)
    ppermute x6, waiting for transfers between devices, shifted(): return lax.ppermute(block, axis, route)  199 us
    all_gather x3, waiting for transfers between devices, body(): lax.all_gather(needed, 'panel', axis=1, tiled=True)  29.1 us
    all_gather x3, waiting for transfers between devices, body(): lax.all_gather(own_gain, 'panel', axis=0, tiled=True)  21.4 us
    dot_general x3, matrix products, times_transposed(): lax.dot_general(left, right, (((1,), (1,)), ((), ())), preferred_element_...  15.5 us
    ppermute x6, starting transfers between devices, shifted(): return lax.ppermute(block, axis, route)  9.38 us
  transfers between devices with their start and end apart: 12, of which 10 were waited for; matrix products, arithmetic and copies ran while one was open for 4% of the time, Pallas kernels for 0%

commit v1 on v0

v1 whole, which is shorter than its diff:
```python
import functools

import jax
import jax.numpy as jnp
from jax import lax
from jax.experimental import pallas as pl
from jax.experimental.pallas import tpu as pltpu
from jax.sharding import PartitionSpec as P

OWNED = (((0, 0), (0, 1), (1, 1), (1, 2), (0, 2)), ((0, 0), (0, 1), (1, 1), (1, 2), (1, 3)))
CHUNKS = 4


def block_table():
    table = {}
    for core in range(2):
        for slot, (row, col) in enumerate(OWNED[core]):
            table[(2 * core + row, (2 * core + col) % 4)] = (core, slot)
    return table


TABLE = block_table()


def dot(a, b):
    return jnp.dot(a, b, preferred_element_type=jnp.float32)


def dot_t(a, b):
    return lax.dot_general(a, b, (((1,), (1,)), ((), ())), preferred_element_type=jnp.float32)


def to_tile(row):
    lanes = row.shape[1] // 8
    return jnp.concatenate([row[:, i * lanes : (i + 1) * lanes] for i in range(8)], axis=0)


def to_row(tile):
    return jnp.concatenate([tile[i : i + 1, :] for i in range(8)], axis=1)


def kernel(
    steps, gain, offset, cov, mean_out, cov_out,
    own, far, weight, near_cov, chain_cov, near_g, chain_g, sent_g, cross, added, added_g,
    s_own, r_own, s_far, r_far, s_farx, r_farx, s_near, r_near, s_nearx, r_nearx,
    s_prod, r_prod, s_chain, r_chain, s_chainx, r_chainx, s_side,
):
    t = lax.axis_index("tm")
    c = lax.axis_index("panel")
    z = t // 2
    y = t % 2
    last_z = steps // 2 - 1
    width = gain.shape[1]
    half = width // 2
    bs = width // 4
    cr = half // CHUNKS

    core = {"panel": 1 - c}
    side = {"tm": t + 1 - 2 * y}
    above = {"tm": t + 2}
    below = {"tm": t - 2}

    barrier = pltpu.get_barrier_semaphore()
    even = y == 0
    top = z == last_z
    pl.semaphore_signal(barrier, inc=1, device_id=core)
    pl.semaphore_signal(barrier, inc=1, device_id=side)

    @pl.when(jnp.logical_and(even, z < last_z))
    def _():
        pl.semaphore_signal(barrier, inc=1, device_id=above)

    @pl.when(jnp.logical_and(even, z > 0))
    def _():
        pl.semaphore_signal(barrier, inc=1, device_id=below)

    has_above = jnp.where(jnp.logical_and(even, z < last_z), 1, 0)
    has_below = jnp.where(jnp.logical_and(even, z > 0), 1, 0)
    pl.semaphore_wait(barrier, 2 + has_above + has_below)

    def remote(src, dst, send, recv, device):
        return pltpu.make_async_remote_copy(
            src_ref=src, dst_ref=dst, send_sem=send, recv_sem=recv,
            device_id=device, device_id_type=pl.DeviceIdType.MESH,
        )

    def cut(ref, slot):
        if OWNED[0][slot] == OWNED[1][slot]:
            row, col = OWNED[0][slot]
        else:
            (r0, c0), (r1, c1) = OWNED[0][slot], OWNED[1][slot]
            row, col = r0 + (r1 - r0) * c, c0 + (c1 - c0) * c
        start = pl.multiple_of(((col + 2 * c) % 4) * bs, bs)
        return ref.at[pl.ds(pl.multiple_of(row * bs, bs), bs), pl.ds(start, bs)]

    def far_copy(i):
        rows = pl.ds(i * cr, cr)
        return remote(gain.at[rows], far.at[c, rows], s_far.at[i], r_far.at[i], side)

    def far_cross(i, slot):
        rows = pl.ds(i * cr, cr)
        return remote(far.at[slot, rows], far.at[slot, rows], s_farx.at[i], r_farx.at[i], core)

    def near_copy(b):
        return remote(cut(cov, b), near_cov.at[c, b], s_near.at[b], r_near.at[b], side)

    def near_g_copy():
        return remote(sent_g, near_g, s_near.at[5], r_near.at[5], side)

    def near_cross(b, slot):
        return remote(near_cov.at[slot, b], near_cov.at[slot, b], s_nearx.at[b], r_nearx.at[b], core)

    def prod_cross(n, slot):
        cols = pl.ds(n * bs, bs)
        return remote(weight.at[slot, :, cols], weight.at[slot, :, cols], s_prod.at[n], r_prod.at[n], core)

    def chain_copy(b):
        return remote(cut(cov_out, b), chain_cov.at[c, b], s_chain.at[b], r_chain.at[b], below)

    def chain_g_copy():
        return remote(sent_g, chain_g, s_chain.at[5], r_chain.at[5], below)

    def chain_side(b):
        return remote(chain_cov.at[c, b], chain_cov.at[c, b], s_side.at[b], r_chain.at[b], side)

    def chain_g_side():
        return remote(chain_g, chain_g, s_side.at[5], r_chain.at[5], side)

    def chain_cross(b, slot):
        return remote(chain_cov.at[slot, b], chain_cov.at[slot, b], s_chainx.at[b], r_chainx.at[b], core)

    def combine(left, left_rows, later, later_g, emit, emit_g):
        for j in range(4):
            total = None
            for i in range(4):
                piece = left_rows[:, i * bs : (i + 1) * bs]
                if (i, j) in TABLE:
                    term = dot(piece, later[TABLE[(i, j)]])
                else:
                    term = dot_t(piece, later[TABLE[(j, i)]])
                total = term if total is None else total + term
            cross[:half, j * bs : (j + 1) * bs] = total.astype(jnp.bfloat16)
        row = to_row(later_g[...]).astype(jnp.bfloat16)
        cross[half:, :] = jnp.broadcast_to(row, (16, width))
        for n in range(4):
            panel = (n // 2 + c) % 2
            cols = pl.ds(pl.multiple_of(((n + 2 * c) % 4) * bs, bs), bs)
            rows = left[panel, (n % 2) * bs : (n % 2 + 1) * bs, :]
            out = dot_t(cross[...], rows)
            emit(n, cols, out[:half])
            emit_g(cols, out[half : half + 1])

    def finish(left, left_rows, later, later_g, add, add_g):
        go_down = jnp.logical_and(even, z > 0)

        def emit(n, cols, value):
            cov_out[:, cols] = (value + add(cols)).astype(jnp.bfloat16)
            ready = ((0,), (1, 2), (3,), (4,))[n]

            @pl.when(go_down)
            def _():
                for b in ready:
                    chain_copy(b).start()

        def emit_g(cols, value):
            added_g[:, cols] = value + add_g(cols)

        combine(left, left_rows, later, later_g, emit, emit_g)
        mean_out[...] = added_g[...].astype(jnp.bfloat16)

        @pl.when(go_down)
        def _():
            sent_g[...] = to_tile(added_g[...])
            chain_g_copy().start()
            for b in range(5):
                chain_copy(b).wait_send()
            chain_g_copy().wait_send()

    @pl.when(y == 1)
    def _():
        sent_g[...] = to_tile(offset[...].astype(jnp.float32))

        @pl.when(z < last_z)
        def _():
            for i in range(CHUNKS):
                far_copy(i).start()

        for b in range(5):
            near_copy(b).start()
        near_g_copy().start()

        @pl.when(top)
        def _():
            cov_out[...] = cov[...]
            mean_out[...] = offset[...]

        @pl.when(z < last_z)
        def _():
            swap = remote(gain, weight.at[c], s_own.at[0], r_own.at[0], core)
            swap.start()
            weight[c] = gain[...]
            added[...] = cov[...].astype(jnp.float32)
            added_g[...] = offset[...].astype(jnp.float32)
            swap.wait()

    @pl.when(even)
    def _():
        swap = remote(gain, own.at[c], s_own.at[0], r_own.at[0], core)
        swap.start()
        own[c] = gain[...]

        @pl.when(z < last_z)
        def _():
            for i in range(CHUNKS):
                far_copy(i).wait_recv()
                far_cross(i, c).start()
            for i in range(CHUNKS):
                far_cross(i, 1 - c).wait_recv()
            for n in range(4):
                cols = slice(n * bs, (n + 1) * bs)
                value = dot(gain[:, :half], far[0, :, cols]) + dot(gain[:, half:], far[1, :, cols])
                weight[c, :, cols] = value.astype(jnp.bfloat16)
                prod_cross(n, c).start()

        swap.wait()
        for b in range(5):
            near_copy(b).wait_recv()
            near_cross(b, c).start()
        near_g_copy().wait_recv()
        for b in range(5):
            near_cross(b, 1 - c).wait_recv()

        @pl.when(z < last_z)
        def _():
            def emit(n, cols, value):
                added[:, cols] = value + cov[:, cols].astype(jnp.float32)

            def emit_g(cols, value):
                added_g[:, cols] = value + offset[:, cols].astype(jnp.float32)

            combine(own, gain[...], near_cov, near_g, emit, emit_g)

        @pl.when(top)
        def _():
            finish(
                own, gain[...], near_cov, near_g,
                lambda cols: cov[:, cols].astype(jnp.float32),
                lambda cols: offset[:, cols].astype(jnp.float32),
            )

    @pl.when(z < last_z)
    def _():
        for b in range(5):
            chain_copy(b).wait_recv()
            chain_cross(b, c).start()

            @pl.when(even)
            def _():
                chain_side(b).start()

        chain_g_copy().wait_recv()

        @pl.when(even)
        def _():
            chain_g_side().start()
            for n in range(4):
                prod_cross(n, 1 - c).wait_recv()

        for b in range(5):
            chain_cross(b, 1 - c).wait_recv()
        finish(
            weight, weight[c], chain_cov, chain_g,
            lambda cols: added[:, cols], lambda cols: added_g[:, cols],
        )
        for b in range(5):
            chain_cross(b, c).wait_send()

        @pl.when(even)
        def _():
            for b in range(5):
                chain_side(b).wait_send()
            chain_g_side().wait_send()
            for n in range(4):
                prod_cross(n, c).wait_send()
            for i in range(CHUNKS):
                far_cross(i, c).wait_send()

        @pl.when(y == 1)
        def _():
            for i in range(CHUNKS):
                far_copy(i).wait_send()

    @pl.when(y == 1)
    def _():
        for b in range(5):
            near_copy(b).wait_send()
        near_g_copy().wait_send()

    @pl.when(even)
    def _():
        for b in range(5):
            near_cross(b, c).wait_send()


def body(gain, offset, residual_cov):
    steps = lax.axis_size("tm")
    _, half, width = gain.shape
    bs = width // 4
    bf16, f32 = jnp.bfloat16, jnp.float32
    vmem = pl.BlockSpec(memory_space=pltpu.VMEM)
    counts = (1, 1, CHUNKS, CHUNKS, CHUNKS, CHUNKS, 6, 6, 5, 5, 4, 4, 6, 6, 5, 5, 6)
    mean, cov = pl.pallas_call(
        functools.partial(kernel, steps),
        out_shape=(
            jax.ShapeDtypeStruct((1, width), bf16),
            jax.ShapeDtypeStruct((half, width), bf16),
        ),
        in_specs=[vmem] * 3,
        out_specs=(vmem, vmem),
        scratch_shapes=[
            pltpu.VMEM((2, half, width), bf16),
            pltpu.VMEM((2, half, width), bf16),
            pltpu.VMEM((2, half, width), bf16),
            pltpu.VMEM((2, 5, bs, bs), bf16),
            pltpu.VMEM((2, 5, bs, bs), bf16),
            pltpu.VMEM((8, width // 8), f32),
            pltpu.VMEM((8, width // 8), f32),
            pltpu.VMEM((8, width // 8), f32),
            pltpu.VMEM((half + 16, width), bf16),
            pltpu.VMEM((half, width), f32),
            pltpu.VMEM((1, width), f32),
        ]
        + [pltpu.SemaphoreType.DMA((n,)) for n in counts],
        compiler_params=pltpu.CompilerParams(
            collective_id=0, has_side_effects=True, vmem_limit_bytes=40 * 2**20
        ),
        cost_estimate=pl.CostEstimate(
            flops=10 * half * width * width, bytes_accessed=6 * half * width, transcendentals=0
        ),
    )(gain[0], offset, residual_cov[0])
    return mean, cov[None]


def solution(mesh):
    in_specs = (
        P(("parts", "tm"), "panel", None),
        P(("parts", "tm"), None),
        P(("parts", "tm"), "panel", None),
    )
    out_specs = (P(("parts", "tm"), None), P(("parts", "tm"), "panel", None))
    return jax.shard_map(body, mesh=mesh, in_specs=in_specs, out_specs=out_specs, check_vma=False)
```

time: 315 us -> 97.9 us (0.31); the launches traced: 311 us -> 97.6 us
  waiting for transfers between devices: 251 us -> 0 us
  Pallas kernels: 0 us -> 92.3 us
  matrix products: 24.9 us -> 0 us
  between operations: 14.3 us -> 0.65 us
  starting transfers between devices: 9.62 us -> 0 us
  other arithmetic: 4.74 us -> 0 us
    ppermute x6 -> x0, waiting for transfers between devices: 199 us -> none  [shifted(): return lax.ppermute(block, axis, route)]
    pallas_call x0 -> x1, Pallas kernels: none -> 92.3 us  [body(): pl.pallas_call(functools.partial(kernel, steps), out_shape=(jax.ShapeDtyp...]
    all_gather x6 -> x0, waiting for transfers between devices: 50.4 us -> none  [the longest x3 29.1 us: body(): lax.all_gather(needed, 'panel', axis=1, tiled=True)]
    dot_general x8 -> x0, matrix products: 24.9 us -> none  [the longest x3 15.5 us: times_transposed(): lax.dot_general(left, right, (((1,), (1,)), ((), ())), preferred_element_...]
    ppermute x6 -> x0, starting transfers between devices: 9.38 us -> none  [shifted(): return lax.ppermute(block, axis, route)]
    another operation x3 -> x0, other arithmetic: 3.32 us -> none  [body(): jnp.stack([own_gain, own_cov])]
  transfers between devices with their start and end apart: 12 -> 0, of which waited for: 10 -> 0; matrix products, arithmetic and copies ran while one was open for 4% -> 0% of each run, Pallas kernels for 0% -> 0%
where the time goes in v1:
time: 97.9 us; the launch traced here: 97.6 us
  Pallas kernels  92.3 us (94%)
  local copies, waits for them, and re-layouts  4.69 us (5%)
    pallas_call x1, Pallas kernels, body(): pl.pallas_call(functools.partial(kernel, steps), out_shape=(jax.ShapeDtyp...  92.3 us
    unnamed x8, local copies, waits for them, and re-layouts  4.69 us

profile of v1, /device:TPU:5, one launch (start us, length us, event | category | flops | bytes accessed | tf_op | source)
XLA Modules:
  0.0 97.6 jit_solution(5759468273318506145)
XLA Ops:
  0.6 0.0 copy-start
  0.6 1.2 %copy-done = bf16[1,512,1024]{2,1,0:T(8,128)(2,1)S(1)} copy-done((bf16[1,512,1024]{2,1,0:T(8,128)(2,1)S(1)}, bf16[1,512,1024]{2,1,0:T(8,128)(2,1)}, u32[]{:S(2)}) %copy-start) | copy-done | bytes 1048600
  1.9 0.0 copy-start.1
  1.9 1.2 %copy-done.1 = bf16[1,512,1024]{2,1,0:T(8,128)(2,1)S(1)} copy-done((bf16[1,512,1024]{2,1,0:T(8,128)(2,1)S(1)}, bf16[1,512,1024]{2,1,0:T(8,128)(2,1)}, u32[]{:S(2)}) %copy-start.1) | copy-done | bytes 1048600
  3.1 0.0 copy-start.2
  3.1 0.7 copy-done.2
  3.8 92.3 %shard_map.50 = (bf16[1,1024]{1,0:T(2,128)(2,1)S(1)}, bf16[512,1024]{1,0:T(8,128)(2,1)S(1)}) custom-call(bf16[512,1024]{1,0:T(8,128)(2,1)S(1)} %bitcast.4, bf16[1,1024]{1,0:T(2,128)(2,1)S(1)} %copy-done.2, bf16[512,1024]{1,0:T(8,128)(2,1)S(1)} %bitcast.5), custom_call_target="tpu_custom_call" | custom-call | flops 5368709120 | bytes 3145728 | tf_op jit(solution)/shard_map/pallas_call | solution.py:312
  96.1 0.6 copy.7
  96.7 1.0 copy.8
Async XLA Ops:
  0.6 1.2 %copy-start = (bf16[1,512,1024]{2,1,0:T(8,128)(2,1)S(1)}, bf16[1,512,1024]{2,1,0:T(8,128)(2,1)}, u32[]{:S(2)}) copy-start(bf16[1,512,1024]{2,1,0:T(8,128)(2,1)} %param.3) | copy-start | bytes 3145732
  1.9 1.2 %copy-start.1 = (bf16[1,512,1024]{2,1,0:T(8,128)(2,1)S(1)}, bf16[1,512,1024]{2,1,0:T(8,128)(2,1)}, u32[]{:S(2)}) copy-start(bf16[1,512,1024]{2,1,0:T(8,128)(2,1)} %param.5) | copy-start | bytes 3145732
  3.1 0.7 copy-start.2

commit v2 on v1

v2 whole, which is shorter than its diff:
```python
import functools

import jax
import jax.numpy as jnp
from jax import lax
from jax.experimental import pallas as pl
from jax.experimental.pallas import tpu as pltpu
from jax.sharding import PartitionSpec as P

OWNED = (((0, 0), (0, 1), (1, 1), (1, 2), (0, 2)), ((0, 0), (0, 1), (1, 1), (1, 2), (1, 3)))
CHUNKS = 4
UNITS = 10
DIAGONAL = (0, 2)
ROUND = (0, 1, 2, 3)
DIRECT = (4, 5, 6, 7, 8, 9)
EVEN_ORDER = (4, 5, 6, 0, 7, 1, 8, 2, 9, 3)
ODD_ORDER = (0, 1, 4, 2, 5, 3, 6, 7, 8, 9)


def block_table():
    table = {}
    for core in range(2):
        for slot, (row, col) in enumerate(OWNED[core]):
            table[(2 * core + row, (2 * core + col) % 4)] = (core, slot)
    return table


TABLE = block_table()


def dot(a, b):
    return jnp.dot(a, b, preferred_element_type=jnp.float32)


def dot_t(a, b):
    return lax.dot_general(a, b, (((1,), (1,)), ((), ())), preferred_element_type=jnp.float32)


def to_tile(row):
    lanes = row.shape[1] // 8
    return jnp.concatenate([row[:, i * lanes : (i + 1) * lanes] for i in range(8)], axis=0)


def to_row(tile):
    return jnp.concatenate([tile[i : i + 1, :] for i in range(8)], axis=1)


def kernel(
    steps, gain_in, offset, cov_in, mean_out, cov_out,
    own, far, weight, near_cov, chain_cov, relay_cov, cov,
    near_g, chain_g, sent_g, cross, added, added_g,
    s_local, s_own, r_own, s_far, r_far, s_farx, r_farx, s_near, r_near, s_nearx, r_nearx,
    s_prod, r_prod, s_chain, r_chain, s_chainx, r_chainx, s_side, s_relay, r_relay,
):
    t = lax.axis_index("tm")
    c = lax.axis_index("panel")
    z = t // 2
    y = t % 2
    last_z = steps // 2 - 1
    half, width = cov.shape
    bs = width // 4
    hb = bs // 2
    cr = half // CHUNKS

    core = {"panel": 1 - c}
    side = {"tm": t + 1 - 2 * y}
    above = {"tm": t + 2}
    below = {"tm": t - 2}
    even = y == 0
    odd = y == 1
    top = z == last_z
    second = z == last_z - 1

    load_cov = pltpu.make_async_copy(cov_in, cov, s_local.at[0])
    load_cov.start()

    @pl.when(even)
    def _():
        pltpu.make_async_copy(gain_in, own.at[c], s_local.at[1]).start()

    @pl.when(odd)
    def _():
        pltpu.make_async_copy(gain_in, weight.at[c], s_local.at[1]).start()

    barrier = pltpu.get_barrier_semaphore()
    pl.semaphore_signal(barrier, inc=1, device_id=core)
    pl.semaphore_signal(barrier, inc=1, device_id=side)

    @pl.when(z < last_z)
    def _():
        pl.semaphore_signal(barrier, inc=1, device_id=above)

    @pl.when(z > 0)
    def _():
        pl.semaphore_signal(barrier, inc=1, device_id=below)

    pl.semaphore_wait(barrier, 2 + jnp.where(z < last_z, 1, 0) + jnp.where(z > 0, 1, 0))

    def remote(src, dst, send, recv, device):
        return pltpu.make_async_remote_copy(
            src_ref=src, dst_ref=dst, send_sem=send, recv_sem=recv,
            device_id=device, device_id_type=pl.DeviceIdType.MESH,
        )

    def skipped(u):
        return hb if u // 2 in DIAGONAL and u % 2 == 1 else 0

    def cut(ref, u):
        slot, low = u // 2, u % 2
        (r0, c0), (r1, c1) = OWNED[0][slot], OWNED[1][slot]
        row = r0 if r0 == r1 else r0 + (r1 - r0) * c
        col = c0 if c0 == c1 else c0 + (c1 - c0) * c
        skip = skipped(u)
        start = pl.multiple_of(((col + 2 * c) % 4) * bs + skip, hb)
        return ref.at[pl.ds(pl.multiple_of(row * bs + low * hb, hb), hb), pl.ds(start, bs - skip)]

    def unit(ref, owner, u):
        skip = skipped(u)
        return ref.at[owner, u // 2, pl.ds(u % 2 * hb, hb), pl.ds(skip, bs - skip)]

    def relay_unit(u):
        skip = skipped(u)
        return relay_cov.at[u // 2, pl.ds(u % 2 * hb, hb), pl.ds(skip, bs - skip)]

    def far_copy(i):
        rows = pl.ds(i * cr, cr)
        return remote(gain_in.at[rows], far.at[c, rows], s_far.at[i], r_far.at[i], side)

    def far_cross(i, slot):
        rows = pl.ds(i * cr, cr)
        return remote(far.at[slot, rows], far.at[slot, rows], s_farx.at[i], r_farx.at[i], core)

    def near_copy(u):
        return remote(cut(cov_in, u), unit(near_cov, c, u), s_near.at[u], r_near.at[u], side)

    def near_g_copy():
        return remote(sent_g, near_g, s_near.at[UNITS], r_near.at[UNITS], side)

    def near_cross(u, owner):
        part = unit(near_cov, owner, u)
        return remote(part, part, s_nearx.at[u], r_nearx.at[u], core)

    def prod_cross(n, slot):
        cols = pl.ds(n * bs, bs)
        return remote(weight.at[slot, :, cols], weight.at[slot, :, cols], s_prod.at[n], r_prod.at[n], core)

    def chain_copy(u):
        return remote(cut(cov_out, u), unit(chain_cov, c, u), s_chain.at[u], r_chain.at[u], below)

    def relay_copy(u):
        return remote(cut(cov_out, u), relay_unit(u), s_chain.at[u], r_relay.at[u], side)

    def relay_down(u):
        return remote(relay_unit(u), unit(chain_cov, c, u), s_relay.at[u], r_chain.at[u], below)

    def chain_g_copy():
        return remote(sent_g, chain_g, s_chain.at[UNITS], r_chain.at[UNITS], below)

    def chain_side(u):
        part = unit(chain_cov, c, u)
        return remote(part, part, s_side.at[u], r_chain.at[u], side)

    def chain_g_side():
        return remote(chain_g, chain_g, s_side.at[UNITS], r_chain.at[UNITS], side)

    def chain_cross(u, owner):
        part = unit(chain_cov, owner, u)
        return remote(part, part, s_chainx.at[u], r_chainx.at[u], core)

    def combine(left, later, later_g, emit, emit_g):
        for owner in range(2):
            for slot in DIAGONAL:
                later[owner, slot, hb:, :hb] = later[owner, slot, :hb, hb:].T
        for j in range(4):
            total = None
            for i in range(4):
                piece = left[c, :, i * bs : (i + 1) * bs]
                if (i, j) in TABLE:
                    term = dot(piece, later[TABLE[(i, j)]])
                else:
                    term = dot_t(piece, later[TABLE[(j, i)]])
                total = term if total is None else total + term
            cross[:half, j * bs : (j + 1) * bs] = total.astype(jnp.bfloat16)
        row = to_row(later_g[...]).astype(jnp.bfloat16)
        cross[half:, :] = jnp.broadcast_to(row, (16, width))
        for n in range(4):
            panel = (n // 2 + c) % 2
            cols = pl.ds(pl.multiple_of(((n + 2 * c) % 4) * bs, bs), bs)
            rows = left[panel, (n % 2) * bs : (n % 2 + 1) * bs, :]
            out = dot_t(cross[...], rows)
            emit(n, cols, out[:half])
            emit_g(cols, out[half : half + 1])

    def first(left, later, later_g):
        def emit(n, cols, value):
            added[:, cols] = value + cov[:, cols].astype(jnp.float32)

        def emit_g(cols, value):
            added_g[:, cols] = value + offset[:, cols].astype(jnp.float32)

        combine(left, later, later_g, emit, emit_g)

    def finish(left, later, later_g):
        go_down = jnp.logical_and(even, z > 0)
        around = jnp.logical_and(go_down, z < last_z)
        straight = jnp.logical_and(go_down, top)

        def emit(n, cols, value):
            cov_out[:, cols] = (value + added[:, cols]).astype(jnp.bfloat16)
            ready = [2 * slot + low for slot in ((0,), (1, 2), (3,), (4,))[n] for low in range(2)]

            @pl.when(around)
            def _():
                for u in ready:
                    (relay_copy(u) if u in ROUND else chain_copy(u)).start()

            @pl.when(straight)
            def _():
                for u in ready:
                    chain_copy(u).start()

        def emit_g(cols, value):
            added_g[:, cols] = value + added_g[:, cols]

        combine(left, later, later_g, emit, emit_g)
        mean_out[...] = added_g[...].astype(jnp.bfloat16)

        @pl.when(go_down)
        def _():
            sent_g[...] = to_tile(added_g[...])
            chain_g_copy().start()
            for u in range(UNITS):
                chain_copy(u).wait_send()
            chain_g_copy().wait_send()

    def plain_added():
        added[...] = cov[...].astype(jnp.float32)
        added_g[...] = offset[...].astype(jnp.float32)

    def receive(order, forwarded):
        for u in order:
            chain_copy(u).wait_recv()
            chain_cross(u, c).start()
            if u in forwarded:
                chain_side(u).start()

    def receive_near(units):
        for u in units:
            near_copy(u).wait_recv()
            near_cross(u, c).start()

    @pl.when(odd)
    def _():
        sent_g[...] = to_tile(offset[...].astype(jnp.float32))

        @pl.when(z < last_z)
        def _():
            for i in range(CHUNKS):
                far_copy(i).start()

        for u in range(UNITS):
            near_copy(u).start()
        near_g_copy().start()
        load_cov.wait()
        pltpu.make_async_copy(gain_in, weight.at[c], s_local.at[1]).wait()

        @pl.when(top)
        def _():
            cov_out[...] = cov[...]
            mean_out[...] = offset[...]

        @pl.when(z < last_z)
        def _():
            swap = remote(gain_in, weight.at[c], s_own.at[0], r_own.at[0], core)
            swap.start()
            plain_added()
            swap.wait()

            @pl.when(second)
            def _():
                receive(range(UNITS), ())

            @pl.when(jnp.logical_not(second))
            def _():
                receive(ODD_ORDER, ROUND)

            chain_g_copy().wait_recv()

            @pl.when(z > 0)
            def _():
                for u in ROUND:
                    relay_copy(u).wait_recv()
                    relay_down(u).start()

    @pl.when(even)
    def _():
        swap = remote(gain_in, own.at[c], s_own.at[0], r_own.at[0], core)
        swap.start()
        load_cov.wait()
        pltpu.make_async_copy(gain_in, own.at[c], s_local.at[1]).wait()

        @pl.when(z < last_z)
        def _():
            for i in range(CHUNKS):
                far_copy(i).wait_recv()
                far_cross(i, c).start()
            for i in range(CHUNKS):
                far_cross(i, 1 - c).wait_recv()
            for n in range(4):
                cols = slice(n * bs, (n + 1) * bs)
                value = dot(own[c, :, :half], far[0, :, cols]) + dot(own[c, :, half:], far[1, :, cols])
                weight[c, :, cols] = value.astype(jnp.bfloat16)
                prod_cross(n, c).start()

        swap.wait()

        @pl.when(second)
        def _():
            receive(range(UNITS), range(UNITS))
            chain_g_copy().wait_recv()
            chain_g_side().start()
            receive_near(range(5))
            for n in range(4):
                prod_cross(n, 1 - c).wait_recv()
            for u in range(UNITS):
                chain_cross(u, 1 - c).wait_recv()
            first(weight, chain_cov, chain_g)
            receive_near(range(5, UNITS))

        @pl.when(jnp.logical_not(second))
        def _():
            receive_near(range(UNITS))

        near_g_copy().wait_recv()
        for u in range(UNITS):
            near_cross(u, 1 - c).wait_recv()

        @pl.when(z < last_z - 1)
        def _():
            first(own, near_cov, near_g)
            receive(EVEN_ORDER, DIRECT)
            chain_g_copy().wait_recv()
            chain_g_side().start()
            for n in range(4):
                prod_cross(n, 1 - c).wait_recv()

        @pl.when(top)
        def _():
            plain_added()

        @pl.when(z >= last_z - 1)
        def _():
            finish(own, near_cov, near_g)

    @pl.when(jnp.logical_or(z < last_z - 1, jnp.logical_and(odd, second)))
    def _():
        for u in range(UNITS):
            chain_cross(u, 1 - c).wait_recv()
        finish(weight, chain_cov, chain_g)

    @pl.when(z < last_z)
    def _():
        for u in range(UNITS):
            chain_cross(u, c).wait_send()

    @pl.when(even)
    def _():
        for u in range(UNITS):
            near_cross(u, c).wait_send()

        @pl.when(z < last_z)
        def _():
            chain_g_side().wait_send()
            for u in DIRECT:
                chain_side(u).wait_send()
            for n in range(4):
                prod_cross(n, c).wait_send()
            for i in range(CHUNKS):
                far_cross(i, c).wait_send()

        @pl.when(second)
        def _():
            for u in ROUND:
                chain_side(u).wait_send()

    @pl.when(odd)
    def _():
        for u in range(UNITS):
            near_copy(u).wait_send()
        near_g_copy().wait_send()

        @pl.when(z < last_z)
        def _():
            for i in range(CHUNKS):
                far_copy(i).wait_send()

            @pl.when(z > 0)
            def _():
                for u in ROUND:
                    relay_down(u).wait_send()

        @pl.when(z < last_z - 1)
        def _():
            for u in ROUND:
                chain_side(u).wait_send()


def body(gain, offset, residual_cov):
    steps = lax.axis_size("tm")
    _, half, width = gain.shape
    bs = width // 4
    bf16, f32 = jnp.bfloat16, jnp.float32
    hbm = pl.BlockSpec(memory_space=pl.ANY)
    vmem = pl.BlockSpec(memory_space=pltpu.VMEM)
    counts = (2, 1, 1) + (CHUNKS,) * 4 + (UNITS + 1,) * 4 + (4, 4) + (UNITS + 1,) * 7
    mean, cov = pl.pallas_call(
        functools.partial(kernel, steps),
        out_shape=(
            jax.ShapeDtypeStruct((1, width), bf16),
            jax.ShapeDtypeStruct((half, width), bf16),
        ),
        in_specs=[hbm, vmem, hbm],
        out_specs=(vmem, vmem),
        scratch_shapes=[
            pltpu.VMEM((2, half, width), bf16),
            pltpu.VMEM((2, half, width), bf16),
            pltpu.VMEM((2, half, width), bf16),
            pltpu.VMEM((2, 5, bs, bs), bf16),
            pltpu.VMEM((2, 5, bs, bs), bf16),
            pltpu.VMEM((2, bs, bs), bf16),
            pltpu.VMEM((half, width), bf16),
            pltpu.VMEM((8, width // 8), f32),
            pltpu.VMEM((8, width // 8), f32),
            pltpu.VMEM((8, width // 8), f32),
            pltpu.VMEM((half + 16, width), bf16),
            pltpu.VMEM((half, width), f32),
            pltpu.VMEM((1, width), f32),
        ]
        + [pltpu.SemaphoreType.DMA((n,)) for n in counts],
        compiler_params=pltpu.CompilerParams(
            collective_id=0, has_side_effects=True, vmem_limit_bytes=40 * 2**20
        ),
        cost_estimate=pl.CostEstimate(
            flops=10 * half * width * width, bytes_accessed=6 * half * width, transcendentals=0
        ),
    )(gain[0], offset, residual_cov[0])
    return mean, cov[None]


def solution(mesh):
    in_specs = (
        P(("parts", "tm"), "panel", None),
        P(("parts", "tm"), None),
        P(("parts", "tm"), "panel", None),
    )
    out_specs = (P(("parts", "tm"), None), P(("parts", "tm"), "panel", None))
    return jax.shard_map(body, mesh=mesh, in_specs=in_specs, out_specs=out_specs, check_vma=False)
```

time: 97.9 us -> 88.8 us (0.907)
  Pallas kernels: 92.3 us -> 83.3 us
    pallas_call x1, Pallas kernels: 92.3 us -> 83.3 us  [body(): pl.pallas_call(functools.partial(kernel, steps), out_shape=(jax.ShapeDtyp...]
where the time goes in v2:
time: 88.8 us; the launch traced here: 88.6 us
  Pallas kernels  83.3 us (94%)
  local copies, waits for them, and re-layouts  4.69 us (5%)
    pallas_call x1, Pallas kernels, body(): pl.pallas_call(functools.partial(kernel, steps), out_shape=(jax.ShapeDtyp...  83.3 us
    unnamed x8, local copies, waits for them, and re-layouts  4.69 us

profile of v2, /device:TPU:5, one launch (start us, length us, event | category | flops | bytes accessed | tf_op | source)
XLA Modules:
  0.0 88.6 jit_solution(1837630221577517006)
XLA Ops:
  0.6 0.0 copy-start
  0.6 1.2 %copy-done = bf16[1,512,1024]{2,1,0:T(8,128)(2,1)S(1)} copy-done((bf16[1,512,1024]{2,1,0:T(8,128)(2,1)S(1)}, bf16[1,512,1024]{2,1,0:T(8,128)(2,1)}, u32[]{:S(2)}) %copy-start) | copy-done | bytes 1048600
  1.9 0.0 copy-start.1
  1.9 1.2 %copy-done.1 = bf16[1,512,1024]{2,1,0:T(8,128)(2,1)S(1)} copy-done((bf16[1,512,1024]{2,1,0:T(8,128)(2,1)S(1)}, bf16[1,512,1024]{2,1,0:T(8,128)(2,1)}, u32[]{:S(2)}) %copy-start.1) | copy-done | bytes 1048600
  3.1 0.0 copy-start.2
  3.1 0.7 copy-done.2
  3.8 83.3 %shard_map.50 = (bf16[1,1024]{1,0:T(2,128)(2,1)S(1)}, bf16[512,1024]{1,0:T(8,128)(2,1)S(1)}) custom-call(bf16[512,1024]{1,0:T(8,128)(2,1)S(1)} %bitcast.4, bf16[1,1024]{1,0:T(2,128)(2,1)S(1)} %copy-done.2, bf16[512,1024]{1,0:T(8,128)(2,1)S(1)} %bitcast.5), custom_call_target="tpu_custom_call" | custom-call | flops 5368709120 | bytes 3145728 | tf_op jit(solution)/shard_map/pallas_call | solution.py:416
  87.0 0.6 copy.7
  87.6 1.0 %copy.8 = bf16[1,512,1024]{2,1,0:T(8,128)(2,1)} copy(bf16[1,512,1024]{2,1,0:T(8,128)(2,1)S(1)} %bitcast.3) | data formatting | bytes 2097152
Async XLA Ops:
  0.6 1.2 %copy-start = (bf16[1,512,1024]{2,1,0:T(8,128)(2,1)S(1)}, bf16[1,512,1024]{2,1,0:T(8,128)(2,1)}, u32[]{:S(2)}) copy-start(bf16[1,512,1024]{2,1,0:T(8,128)(2,1)} %param.3) | copy-start | bytes 3145732
  1.9 1.2 %copy-start.1 = (bf16[1,512,1024]{2,1,0:T(8,128)(2,1)S(1)}, bf16[1,512,1024]{2,1,0:T(8,128)(2,1)}, u32[]{:S(2)}) copy-start(bf16[1,512,1024]{2,1,0:T(8,128)(2,1)} %param.5) | copy-start | bytes 3145732
  3.1 0.7 copy-start.2

commit v3 on v2

--- a/solution.py
+++ b/solution.py
@@ -11,10 +11,11 @@
 CHUNKS = 4
 UNITS = 10
 DIAGONAL = (0, 2)
-ROUND = (0, 1, 2, 3)
-DIRECT = (4, 5, 6, 7, 8, 9)
-EVEN_ORDER = (4, 5, 6, 0, 7, 1, 8, 2, 9, 3)
-ODD_ORDER = (0, 1, 4, 2, 5, 3, 6, 7, 8, 9)
+ROUND = (0, 2)
+DIRECT = (1, 3, 4, 5, 6, 7, 8, 9)
+EVEN_ORDER = (1, 3, 4, 5, 6, 7, 0, 8, 2, 9)
+ODD_ORDER = (0, 1, 2, 3, 4, 5, 6, 7, 8, 9)
+WINDOW = 3
 
 
 def block_table():
@@ -166,6 +167,11 @@
     def chain_cross(u, owner):
         part = unit(chain_cov, owner, u)
         return remote(part, part, s_chainx.at[u], r_chainx.at[u], core)
+
+    def start_in_turn(copy, sequence, k, window=WINDOW):
+        if k >= window:
+            copy(sequence[k - window]).wait_send()
+        copy(sequence[k]).start()
 
     def combine(left, later, later_g, emit, emit_g):
         for owner in range(2):
@@ -212,12 +218,15 @@
             @pl.when(around)
             def _():
                 for u in ready:
-                    (relay_copy(u) if u in ROUND else chain_copy(u)).start()
+                    if u in ROUND:
+                        relay_copy(u).start()
+                    else:
+                        start_in_turn(chain_copy, DIRECT, DIRECT.index(u))
 
             @pl.when(straight)
             def _():
                 for u in ready:
-                    chain_copy(u).start()
+                    start_in_turn(chain_copy, range(UNITS), u)
 
         def emit_g(cols, value):
             added_g[:, cols] = value + added_g[:, cols]
@@ -229,9 +238,17 @@
         def _():
             sent_g[...] = to_tile(added_g[...])
             chain_g_copy().start()
-            for u in range(UNITS):
+            chain_g_copy().wait_send()
+
+        @pl.when(around)
+        def _():
+            for u in ROUND + DIRECT[-WINDOW:]:
                 chain_copy(u).wait_send()
-            chain_g_copy().wait_send()
+
+        @pl.when(straight)
+        def _():
+            for u in range(UNITS)[-WINDOW:]:
+                chain_copy(u).wait_send()
 
     def plain_added():
         added[...] = cov[...].astype(jnp.float32)
@@ -252,30 +269,38 @@
     @pl.when(odd)
     def _():
         sent_g[...] = to_tile(offset[...].astype(jnp.float32))
+        near_g_copy().start()
 
         @pl.when(z < last_z)
         def _():
-            for i in range(CHUNKS):
+            for i in range(2):
                 far_copy(i).start()
-
-        for u in range(UNITS):
-            near_copy(u).start()
-        near_g_copy().start()
-        load_cov.wait()
-        pltpu.make_async_copy(gain_in, weight.at[c], s_local.at[1]).wait()
+            swap = remote(gain_in, weight.at[c], s_own.at[0], r_own.at[0], core)
+            swap.start()
+            load_cov.wait()
+            pltpu.make_async_copy(gain_in, weight.at[c], s_local.at[1]).wait()
+            plain_added()
+            for i in range(2, CHUNKS):
+                start_in_turn(far_copy, range(CHUNKS), i, 2)
+            for i in range(CHUNKS)[-2:]:
+                far_copy(i).wait_send()
+                start_in_turn(near_copy, range(UNITS), i - CHUNKS + 2)
+            swap.wait()
 
         @pl.when(top)
         def _():
+            for u in range(2):
+                near_copy(u).start()
+            load_cov.wait()
+            pltpu.make_async_copy(gain_in, weight.at[c], s_local.at[1]).wait()
             cov_out[...] = cov[...]
             mean_out[...] = offset[...]
 
+        for u in range(2, UNITS):
+            start_in_turn(near_copy, range(UNITS), u)
+
         @pl.when(z < last_z)
         def _():
-            swap = remote(gain_in, weight.at[c], s_own.at[0], r_own.at[0], core)
-            swap.start()
-            plain_added()
-            swap.wait()
-
             @pl.when(second)
             def _():
                 receive(range(UNITS), ())
@@ -385,19 +410,14 @@
 
     @pl.when(odd)
     def _():
-        for u in range(UNITS):
+        for u in range(UNITS)[-WINDOW:]:
             near_copy(u).wait_send()
         near_g_copy().wait_send()
 
-        @pl.when(z < last_z)
-        def _():
-            for i in range(CHUNKS):
-                far_copy(i).wait_send()
-
-            @pl.when(z > 0)
-            def _():
-                for u in ROUND:
-                    relay_down(u).wait_send()
+        @pl.when(jnp.logical_and(z < last_z, z > 0))
+        def _():
+            for u in ROUND:
+                relay_down(u).wait_send()
 
         @pl.when(z < last_z - 1)
         def _():
@@ -410,7 +430,7 @@
     _, half, width = gain.shape
     bs = width // 4
     bf16, f32 = jnp.bfloat16, jnp.float32
-    hbm = pl.BlockSpec(memory_space=pl.ANY)
+    hbm = pl.BlockSpec(memory_space=pltpu.HBM)
     vmem = pl.BlockSpec(memory_space=pltpu.VMEM)
     counts = (2, 1, 1) + (CHUNKS,) * 4 + (UNITS + 1,) * 4 + (4, 4) + (UNITS + 1,) * 7
     mean, cov = pl.pallas_call(

time: 88.8 us -> 86.6 us (0.975)
  Pallas kernels: 83.3 us -> 81 us
    pallas_call x1, Pallas kernels: 83.3 us -> 81 us  [body(): pl.pallas_call(functools.partial(kernel, steps), out_shape=(jax.ShapeDtyp...]
where the time goes in v3:
time: 86.6 us; the launch traced here: 86.4 us
  Pallas kernels  81 us (94%)
  local copies, waits for them, and re-layouts  4.69 us (5%)
    pallas_call x1, Pallas kernels, body(): pl.pallas_call(functools.partial(kernel, steps), out_shape=(jax.ShapeDtyp...  81 us
    unnamed x8, local copies, waits for them, and re-layouts  4.69 us

profile of v3, /device:TPU:5, one launch (start us, length us, event | category | flops | bytes accessed | tf_op | source)
XLA Modules:
  0.0 86.4 jit_solution(16069127734554328522)
XLA Ops:
  0.6 0.0 copy-start
  0.6 1.2 %copy-done = bf16[1,512,1024]{2,1,0:T(8,128)(2,1)S(1)} copy-done((bf16[1,512,1024]{2,1,0:T(8,128)(2,1)S(1)}, bf16[1,512,1024]{2,1,0:T(8,128)(2,1)}, u32[]{:S(2)}) %copy-start) | copy-done | bytes 1048600
  1.9 0.0 copy-start.1
  1.9 1.2 %copy-done.1 = bf16[1,512,1024]{2,1,0:T(8,128)(2,1)S(1)} copy-done((bf16[1,512,1024]{2,1,0:T(8,128)(2,1)S(1)}, bf16[1,512,1024]{2,1,0:T(8,128)(2,1)}, u32[]{:S(2)}) %copy-start.1) | copy-done | bytes 1048600
  3.1 0.0 copy-start.2
  3.1 0.7 copy-done.2
  3.8 81.0 %shard_map.50 = (bf16[1,1024]{1,0:T(2,128)(2,1)S(1)}, bf16[512,1024]{1,0:T(8,128)(2,1)S(1)}) custom-call(bf16[512,1024]{1,0:T(8,128)(2,1)S(1)} %bitcast.4, bf16[1,1024]{1,0:T(2,128)(2,1)S(1)} %copy-done.2, bf16[512,1024]{1,0:T(8,128)(2,1)S(1)} %bitcast.5), custom_call_target="tpu_custom_call" | custom-call | flops 5368709120 | bytes 3145728 | tf_op jit(solution)/shard_map/pallas_call | solution.py:436
  84.8 0.6 copy.7
  85.4 1.0 %copy.8 = bf16[1,512,1024]{2,1,0:T(8,128)(2,1)} copy(bf16[1,512,1024]{2,1,0:T(8,128)(2,1)S(1)} %bitcast.3) | data formatting | bytes 2097152
Async XLA Ops:
  0.6 1.2 %copy-start = (bf16[1,512,1024]{2,1,0:T(8,128)(2,1)S(1)}, bf16[1,512,1024]{2,1,0:T(8,128)(2,1)}, u32[]{:S(2)}) copy-start(bf16[1,512,1024]{2,1,0:T(8,128)(2,1)} %param.3) | copy-start | bytes 3145732
  1.9 1.2 %copy-start.1 = (bf16[1,512,1024]{2,1,0:T(8,128)(2,1)S(1)}, bf16[1,512,1024]{2,1,0:T(8,128)(2,1)}, u32[]{:S(2)}) copy-start(bf16[1,512,1024]{2,1,0:T(8,128)(2,1)} %param.5) | copy-start | bytes 3145732
  3.1 0.7 copy-start.2

commit v4 on v3

--- a/solution.py
+++ b/solution.py
@@ -11,9 +11,9 @@
 CHUNKS = 4
 UNITS = 10
 DIAGONAL = (0, 2)
-ROUND = (0, 2)
-DIRECT = (1, 3, 4, 5, 6, 7, 8, 9)
-EVEN_ORDER = (1, 3, 4, 5, 6, 7, 0, 8, 2, 9)
+ROUND = (0, 1)
+DIRECT = (2, 3, 4, 5, 6, 7, 8, 9)
+EVEN_ORDER = (2, 3, 4, 5, 6, 7, 0, 1, 8, 9)
 ODD_ORDER = (0, 1, 2, 3, 4, 5, 6, 7, 8, 9)
 WINDOW = 3
 
@@ -173,7 +173,7 @@
             copy(sequence[k - window]).wait_send()
         copy(sequence[k]).start()
 
-    def combine(left, later, later_g, emit, emit_g):
+    def combine(left, later, later_g, emit, emit_g, between=None):
         for owner in range(2):
             for slot in DIAGONAL:
                 later[owner, slot, hb:, :hb] = later[owner, slot, :hb, hb:].T
@@ -187,6 +187,8 @@
                     term = dot_t(piece, later[TABLE[(j, i)]])
                 total = term if total is None else total + term
             cross[:half, j * bs : (j + 1) * bs] = total.astype(jnp.bfloat16)
+        if between is not None:
+            between()
         row = to_row(later_g[...]).astype(jnp.bfloat16)
         cross[half:, :] = jnp.broadcast_to(row, (16, width))
         for n in range(4):
@@ -197,14 +199,14 @@
             emit(n, cols, out[:half])
             emit_g(cols, out[half : half + 1])
 
-    def first(left, later, later_g):
+    def first(left, later, later_g, between=None):
         def emit(n, cols, value):
             added[:, cols] = value + cov[:, cols].astype(jnp.float32)
 
         def emit_g(cols, value):
             added_g[:, cols] = value + offset[:, cols].astype(jnp.float32)
 
-        combine(left, later, later_g, emit, emit_g)
+        combine(left, later, later_g, emit, emit_g, between)
 
     def finish(left, later, later_g):
         go_down = jnp.logical_and(even, z > 0)
@@ -349,8 +351,7 @@
                 prod_cross(n, 1 - c).wait_recv()
             for u in range(UNITS):
                 chain_cross(u, 1 - c).wait_recv()
-            first(weight, chain_cov, chain_g)
-            receive_near(range(5, UNITS))
+            first(weight, chain_cov, chain_g, lambda: receive_near(range(5, UNITS)))
 
         @pl.when(jnp.logical_not(second))
         def _():
@@ -458,7 +459,7 @@
         ]
         + [pltpu.SemaphoreType.DMA((n,)) for n in counts],
         compiler_params=pltpu.CompilerParams(
-            collective_id=0, has_side_effects=True, vmem_limit_bytes=40 * 2**20
+            collective_id=0, has_side_effects=True, vmem_limit_bytes=63 * 2**20
         ),
         cost_estimate=pl.CostEstimate(
             flops=10 * half * width * width, bytes_accessed=6 * half * width, transcendentals=0

time: 86.6 us -> 88.3 us (1.020)
  Pallas kernels: 81 us -> 83.9 us
  local copies, waits for them, and re-layouts: 4.69 us -> 3.52 us
    pallas_call x1, Pallas kernels: 81 us -> 83.9 us  [body(): pl.pallas_call(functools.partial(kernel, steps), out_shape=(jax.ShapeDtyp...]
    unnamed x8 -> x4, local copies, waits for them, and re-layouts: 4.69 us -> 3.52 us
where the time goes in v4:
time: 88.3 us; the launch traced here: 88.1 us
  Pallas kernels  83.9 us (95%)
  local copies, waits for them, and re-layouts  3.52 us (4%)
    pallas_call x1, Pallas kernels, body(): pl.pallas_call(functools.partial(kernel, steps), out_shape=(jax.ShapeDtyp...  83.9 us
    unnamed x4, local copies, waits for them, and re-layouts  3.52 us

profile of v4, /device:TPU:5, one launch (start us, length us, event | category | flops | bytes accessed | tf_op | source)
XLA Modules:
  0.0 88.1 jit_solution(11668286896915400918)
XLA Ops:
  0.6 83.9 %shard_map.50 = (bf16[1,1024]{1,0:T(2,128)(2,1)}, bf16[512,1024]{1,0:T(8,128)(2,1)}) custom-call(bf16[512,1024]{1,0:T(8,128)(2,1)} %bitcast.4, bf16[1,1024]{1,0:T(2,128)(2,1)} %offset.1, bf16[512,1024]{1,0:T(8,128)(2,1)} %bitcast.5), custom_call_target="tpu_custom_call" | custom-call | flops 5368709120 | bytes 3145728 | tf_op jit(solution)/shard_map/pallas_call | solution.py:437
  84.6 0.0 copy-start
  84.6 0.7 copy-done
  85.2 0.6 copy.7
  85.8 2.3 %copy.8 = bf16[1,512,1024]{2,1,0:T(8,128)(2,1)} copy(bf16[1,512,1024]{2,1,0:T(8,128)(2,1)} %bitcast.3) | data formatting | bytes 2097152
Async XLA Ops:
  84.6 0.7 copy-start

commit v5 on v3

--- a/solution.py
+++ b/solution.py
@@ -11,9 +11,9 @@
 CHUNKS = 4
 UNITS = 10
 DIAGONAL = (0, 2)
-ROUND = (0, 2)
-DIRECT = (1, 3, 4, 5, 6, 7, 8, 9)
-EVEN_ORDER = (1, 3, 4, 5, 6, 7, 0, 8, 2, 9)
+ROUND = (0, 1)
+DIRECT = (2, 3, 4, 5, 6, 7, 8, 9)
+EVEN_ORDER = (2, 3, 4, 5, 0, 6, 1, 7, 8, 9)
 ODD_ORDER = (0, 1, 2, 3, 4, 5, 6, 7, 8, 9)
 WINDOW = 3
 

time: 86.6 us -> 89 us (1.028)
  Pallas kernels: 81 us -> 83.4 us
    pallas_call x1, Pallas kernels: 81 us -> 83.4 us  [body(): pl.pallas_call(functools.partial(kernel, steps), out_shape=(jax.ShapeDtyp...]
where the time goes in v5:
time: 89 us; the launch traced here: 88.8 us
  Pallas kernels  83.4 us (94%)
  local copies, waits for them, and re-layouts  4.69 us (5%)
    pallas_call x1, Pallas kernels, body(): pl.pallas_call(functools.partial(kernel, steps), out_shape=(jax.ShapeDtyp...  83.4 us
    unnamed x8, local copies, waits for them, and re-layouts  4.69 us

profile of v5, /device:TPU:5, one launch (start us, length us, event | category | flops | bytes accessed | tf_op | source)
XLA Modules:
  0.0 88.8 jit_solution(17900009910905249784)
XLA Ops:
  0.6 0.0 copy-start
  0.6 1.2 %copy-done = bf16[1,512,1024]{2,1,0:T(8,128)(2,1)S(1)} copy-done((bf16[1,512,1024]{2,1,0:T(8,128)(2,1)S(1)}, bf16[1,512,1024]{2,1,0:T(8,128)(2,1)}, u32[]{:S(2)}) %copy-start) | copy-done | bytes 1048600
  1.9 0.0 copy-start.1
  1.9 1.2 %copy-done.1 = bf16[1,512,1024]{2,1,0:T(8,128)(2,1)S(1)} copy-done((bf16[1,512,1024]{2,1,0:T(8,128)(2,1)S(1)}, bf16[1,512,1024]{2,1,0:T(8,128)(2,1)}, u32[]{:S(2)}) %copy-start.1) | copy-done | bytes 1048600
  3.1 0.0 copy-start.2
  3.1 0.7 copy-done.2
  3.8 83.4 %shard_map.50 = (bf16[1,1024]{1,0:T(2,128)(2,1)S(1)}, bf16[512,1024]{1,0:T(8,128)(2,1)S(1)}) custom-call(bf16[512,1024]{1,0:T(8,128)(2,1)S(1)} %bitcast.4, bf16[1,1024]{1,0:T(2,128)(2,1)S(1)} %copy-done.2, bf16[512,1024]{1,0:T(8,128)(2,1)S(1)} %bitcast.5), custom_call_target="tpu_custom_call" | custom-call | flops 5368709120 | bytes 3145728 | tf_op jit(solution)/shard_map/pallas_call | solution.py:436
  87.2 0.6 copy.7
  87.8 1.0 %copy.8 = bf16[1,512,1024]{2,1,0:T(8,128)(2,1)} copy(bf16[1,512,1024]{2,1,0:T(8,128)(2,1)S(1)} %bitcast.3) | data formatting | bytes 2097152
Async XLA Ops:
  0.6 1.2 %copy-start = (bf16[1,512,1024]{2,1,0:T(8,128)(2,1)S(1)}, bf16[1,512,1024]{2,1,0:T(8,128)(2,1)}, u32[]{:S(2)}) copy-start(bf16[1,512,1024]{2,1,0:T(8,128)(2,1)} %param.3) | copy-start | bytes 3145732
  1.9 1.2 %copy-start.1 = (bf16[1,512,1024]{2,1,0:T(8,128)(2,1)S(1)}, bf16[1,512,1024]{2,1,0:T(8,128)(2,1)}, u32[]{:S(2)}) copy-start(bf16[1,512,1024]{2,1,0:T(8,128)(2,1)} %param.5) | copy-start | bytes 3145732
  3.1 0.7 copy-start.2
